TPU v7x, 32 devices: a whole 2x2x4 slice. The times are simulated.
32 devices in a mesh: grp: 2 (over x), site: 16 (over z, y, core).
Axes of the slice: x: 2, y: 2, z: 4, core: 2. Of those that a mesh axis runs over, the one named last changes fastest.
Arguments:
- psi: bfloat16 [128, 128, 128], P(('grp', 'site')), parts along dimension 0, may hold values from -6 to 6
- left_env: bfloat16 [128, 34, 128, 128], P(('grp', 'site')), parts along dimension 0, may hold values from -1 to 2
- right_env: bfloat16 [128, 34, 128, 128], P(('grp', 'site')), parts along dimension 0, may hold values from -2 to 2
- mpo_shift: int32 [34], replicated, may hold values from -1 to 1
- block_sizes: int32 [128, 2], P(('grp', 'site')), parts along dimension 0, may hold values from 64 to 128
Outputs:
- krylov: bfloat16 [128, 128, 128], P(('grp', 'site')), parts along dimension 0
- image: bfloat16 [128, 128, 128], P(('grp', 'site')), parts along dimension 0
- coefficients: float32 [10], P('grp'), parts along dimension 0
There are 2 independent parts, one for each index of `grp`. A program takes and returns all parts, laid end to end along the dimension named above; an argument that names none is the same for every part. Nothing has to cross between parts.
Inputs may be any that keep to these rules, and one draw needn't show every extreme that they name: `mpo_shift`: each MPO index moves the sector by -1, 0 or +1.
All inputs are finite; a program needn't handle non-finite values.
Results may differ from a plain program's by a relative error of at most 0.013.
Values may be sent and summed in bfloat16 or wider, within the bound.
A program may use at most 64 MiB of HBM per device.

v0:
```python
import jax
import jax.numpy as jnp
from jax import lax
from jax.sharding import PartitionSpec as P


def with_halo(cells, sides, width):
    for axis, dim in sides:
        count = lax.axis_size(axis)
        ends = count - 1
        head = lax.slice_in_dim(cells, 0, width, axis=dim)
        tail = lax.slice_in_dim(cells, cells.shape[dim] - width, cells.shape[dim], axis=dim)
        cells = jnp.concatenate(
            [
                lax.ppermute(tail, axis, [(i, (i + 1) % count) for i in range(ends)]),
                cells,
                lax.ppermute(head, axis, [((i + 1) % count, i) for i in range(ends)]),
            ],
            axis=dim,
        )
    return cells


def right_products(vector, envir):
    return jnp.einsum("nij,nwjk->nwik", vector, envir, preferred_element_type=jnp.float32).astype(
        jnp.bfloat16
    )


def shards(psi, left_env, right_env, mpo_shift, block_sizes):
    sectors = psi.shape[0]
    width = psi.shape[1]
    cells = sectors * width * width * lax.axis_size("site")
    positions = jnp.arange(width, dtype=jnp.int32)
    rows_live = positions[None, :] < block_sizes[:, 0:1]
    cols_live = positions[None, :] < block_sizes[:, 1:2]
    live_mask = (rows_live[:, :, None] & cols_live[:, None, :]).astype(jnp.float32)
    shift_low = (mpo_shift == -1)[None, :, None, None]
    shift_mid = (mpo_shift == 0)[None, :, None, None]

    def apply_h(vector):
        extended = with_halo(right_products(vector, right_env), (("site", 0),), 1)
        chosen = jnp.where(
            shift_low,
            extended[:sectors],
            jnp.where(shift_mid, extended[1 : sectors + 1], extended[2 : sectors + 2]),
        )
        return live_mask * jnp.einsum(
            "nwij,nwjk->nik", left_env, chosen, preferred_element_type=jnp.float32
        )

    start = psi.astype(jnp.float32) * live_mask
    scale = jnp.sqrt(lax.psum(jnp.sum(start * start), "site") / cells + 1e-06)
    vector = (start / scale).astype(jnp.bfloat16)
    previous = jnp.zeros(psi.shape, jnp.float32)
    beta = jnp.zeros((), jnp.float32)
    alphas = []
    betas = []
    for step in range(2):
        vector_f = vector.astype(jnp.float32)
        image = apply_h(vector)
        alpha = lax.psum(jnp.sum(vector_f * image), "site") / cells
        residue = image - alpha * vector_f - beta * previous
        square = lax.psum(jnp.sum(residue * residue), "site") / cells
        beta = jnp.sqrt(jnp.maximum(square, 0.0) + 1e-06)
        alphas.append(alpha)
        betas.append(beta)
        previous = vector_f
        vector = (residue / beta).astype(jnp.bfloat16)
    vector_f = vector.astype(jnp.float32)
    image = apply_h(vector)
    alpha_last = lax.psum(jnp.sum(vector_f * image), "site") / cells
    coefficients = jnp.stack([alphas[0], alphas[1], alpha_last, betas[0], betas[1]])
    return (vector, image.astype(jnp.bfloat16), coefficients)


def solution(mesh):
    in_specs = (
        P(("grp", "site"), None, None),
        P(("grp", "site"), None, None, None),
        P(("grp", "site"), None, None, None),
        P(),
        P(("grp", "site"), None),
    )
    out_specs = (P(("grp", "site"), None, None), P(("grp", "site"), None, None), P("grp"))
    return jax.shard_map(shards, mesh=mesh, in_specs=in_specs, out_specs=out_specs, check_vma=False)
```

profile of v0, /device:TPU:0, one launch (start us, length us, event | category | flops | bytes accessed | tf_op | source)
XLA Modules:
  0.0 311.9 jit_solution(9831708177719381073)
XLA Ops:
  0.6 0.8 slice_bitcast_fusion.1
  1.4 1.0 copy.8
  2.4 0.1 iota_compare_fusion
  2.5 0.7 multiply_reduce_fusion.3
  3.2 35.5 %psum.42 = f32[]{:T(128)} all-reduce(f32[]{:T(128)} %multiply_reduce_fusion.3), channel_id=1, replica_groups=mesh['grp'=2,'site'=16] {'site'}, use_global_device_ids=true, to_apply=%region_1.0 | all-reduce | flops 1 | bytes 8 | tf_op jit(solution)/shard_map/psum | solution.py:53
  39.5 3.7 %convert_bitcast_fusion.2 = bf16[4,34,128,128]{3,2,1,0:T(8,128)(2,1)S(1)} fusion(bf16[4,34,128,128]{3,2,1,0:T(8,128)(2,1)} %param.7, bf16[4,128,128]{1,2,0:T(8,128)(2,1)S(1)} %copy.8, f32[]{:T(128)S(6)} %sqrt.9, pred[4,128]{1,0:T(4,128)(4,1)S(1)} %get-tuple-element.23, pred[4,128]{1,0:T(4,128)(4,1)S(1)} %get-tuple-element.24), kind=kOutput, calls=%fused_computation.23 | convolution fusion | flops 572981248 | bytes 9044996 | tf_op jit(solution)/shard_map/nij,nwjk->nwik/dot_general | solution.py:25
  43.2 0.0 copy-start.3
  43.2 0.3 fusion.55
  43.5 2.4 collective-permute-start
  45.8 1.3 collective-permute-start.1
  47.1 0.0 copy-done.3
  47.1 0.1 collective-permute-done
  47.3 3.2 %collective-permute-done.1 = bf16[1,34,128,128]{3,2,1,0:T(8,128)(2,1)S(1)} collective-permute-done((bf16[1,34,128,128]{3,2,1,0:T(8,128)(2,1)S(1)}, bf16[1,34,128,128]{3,2,1,0:T(8,128)(2,1)S(1)}, u32[]{:S(2)}, u32[]{:S(2)}) %collective-permute-start.1) | collective-permute-done | bytes 1114144 | tf_op jit(solution)/shard_map/ppermute | solution.py:17
  50.5 0.0 copy-start.1
  50.5 1.0 copy-done.1
  51.4 6.9 %fusion.45 = (f32[]{:T(128)}, f32[4,128,128]{1,2,0:T(8,128)S(1)}) fusion(f32[]{:T(128)S(6)} %sqrt.9, bf16[4,128,128]{1,2,0:T(8,128)(2,1)S(1)} %copy.8, pred[4,128]{1,0:T(4,128)(4,1)S(1)} %get-tuple-element.23, pred[4,128]{1,0:T(4,128)(4,1)S(1)} %get-tuple-element.24, bf16[4,34,128,128]{3,2,1,0:T(8,128)(2,1)} %param.6, ...), kind=kOutput, calls=%fused_computation.45 | convolution fusion | flops 579928064 | bytes 11535436 | tf_op jit(solution)/shard_map/nwij,nwjk->nik/dot_general | solution.py:48
  58.4 46.6 %psum.43 = f32[]{:T(128)} all-reduce(f32[]{:T(128)} %get-tuple-element.18), channel_id=1, replica_groups=mesh['grp'=2,'site'=16] {'site'}, use_global_device_ids=true, to_apply=%region_3.4 | all-reduce | flops 1 | bytes 8 | tf_op jit(solution)/shard_map/psum | solution.py:62
  105.6 0.7 multiply_reduce_fusion.2
  106.3 30.1 %psum.44 = f32[]{:T(128)} all-reduce(f32[]{:T(128)} %multiply_reduce_fusion.2), channel_id=1, replica_groups=mesh['grp'=2,'site'=16] {'site'}, use_global_device_ids=true, to_apply=%region_5.6 | all-reduce | flops 1 | bytes 8 | tf_op jit(solution)/shard_map/psum | solution.py:64
  137.1 0.1 divide_convert_fusion.1
  137.3 3.6 %convert_bitcast_fusion.1 = bf16[4,34,128,128]{3,2,1,0:T(8,128)(2,1)S(1)} fusion(bf16[4,34,128,128]{3,2,1,0:T(8,128)(2,1)} %param.7, bf16[4,128,128]{1,2,0:T(8,128)(2,1)S(1)} %divide_convert_fusion.1), kind=kOutput, calls=%fused_computation.22 | convolution fusion | flops 572653568 | bytes 9043968 | tf_op jit(solution)/shard_map/nij,nwjk->nwik/dot_general | solution.py:25
  140.9 0.3 fusion.54
  141.2 1.8 collective-permute-start.2
  143.0 1.3 collective-permute-start.3
  144.3 1.0 collective-permute-done.2
  145.3 0.0 copy-start.2
  145.3 1.0 copy-done.2
  146.4 1.4 collective-permute-done.3
  147.8 6.9 %fusion.42 = (f32[]{:T(128)}, f32[4,128,128]{1,2,0:T(8,128)S(1)}) fusion(bf16[4,128,128]{1,2,0:T(8,128)(2,1)S(1)} %divide_convert_fusion.1, bf16[4,34,128,128]{3,2,1,0:T(8,128)(2,1)} %param.6, bf16[4,34,128,128]{3,2,1,0:T(8,128)(2,1)S(1)} %convert_bitcast_fusion.1, bf16[1,34,128,128]{3,2,1,0:T(8,128)(2,1)} %collective-permute-done.3, ...), kind=kOutput, calls=%fused_computation.42 | convolution fusion | flops 579665920 | bytes 11535432 | tf_op jit(solution)/shard_map/nwij,nwjk->nik/dot_general | solution.py:48
  154.7 50.7 %psum.45 = f32[]{:T(128)} all-reduce(f32[]{:T(128)} %get-tuple-element.20), channel_id=1, replica_groups=mesh['grp'=2,'site'=16] {'site'}, use_global_device_ids=true, to_apply=%region_7.8 | all-reduce | flops 1 | bytes 8 | tf_op jit(solution)/shard_map/psum | solution.py:62
  206.1 0.8 multiply_reduce_fusion.1
  206.8 30.1 %psum.46 = f32[]{:T(128)} all-reduce(f32[]{:T(128)} %multiply_reduce_fusion.1), channel_id=1, replica_groups=mesh['grp'=2,'site'=16] {'site'}, use_global_device_ids=true, to_apply=%region_9.10 | all-reduce | flops 1 | bytes 8 | tf_op jit(solution)/shard_map/psum | solution.py:64
  237.6 0.2 divide_convert_fusion
  237.8 3.6 %convert_bitcast_fusion = bf16[4,34,128,128]{3,2,1,0:T(8,128)(2,1)S(1)} fusion(bf16[4,34,128,128]{3,2,1,0:T(8,128)(2,1)} %param.7, bf16[4,128,128]{1,2,0:T(8,128)(2,1)S(1)} %divide_convert_fusion), kind=kOutput, calls=%fused_computation.21 | convolution fusion | flops 572653568 | bytes 9043968 | tf_op jit(solution)/shard_map/nij,nwjk->nwik/dot_general | solution.py:25
  241.4 0.0 copy-start
  241.4 2.0 copy-done
  243.5 0.3 fusion.53
  243.7 2.8 collective-permute-start.4
  246.5 1.5 collective-permute-start.5
  248.0 0.8 copy.15
  248.8 0.0 collective-permute-done.4
  248.8 2.5 collective-permute-done.5
  251.3 9.9 %multiply_reduce_fusion = (f32[]{:T(128)}, bf16[4,128,128]{1,2,0:T(8,128)(2,1)S(1)}) fusion(bf16[4,128,128]{1,2,0:T(8,128)(2,1)S(1)} %divide_convert_fusion, bf16[4,34,128,128]{3,2,1,0:T(8,128)(2,1)} %param.6, bf16[4,34,128,128]{3,2,1,0:T(8,128)(2,1)} %copy-done, bf16[1,34,128,128]{3,2,1,0:T(8,128)(2,1)} %collective-permute-done.5, ...), kind=kOutput, calls=%fused_computation.47 | convolution fusion | flops 579731456 | bytes 11404360 | tf_op jit(solution)/shard_map/nwij,nwjk->nik/dot_general | solution.py:48
  261.2 48.7 %psum.47 = f32[]{:T(128)} all-reduce(f32[]{:T(128)} %get-tuple-element.12), channel_id=1, replica_groups=mesh['grp'=2,'site'=16] {'site'}, use_global_device_ids=true, to_apply=%region_11.12 | all-reduce | flops 1 | bytes 8 | tf_op jit(solution)/shard_map/psum | solution.py:72
  310.5 0.8 copy.16
  311.3 0.6 stack.23
  (1 shorter events, 0.0 us)
Async XLA Ops:
  43.2 3.9 %copy-start.3 = (s32[34]{0:T(128)S(1)}, s32[34]{0:T(128)}, u32[]{:S(2)}) copy-start(s32[34]{0:T(128)} %param.8) | copy-start | bytes 412
  43.5 3.8 %collective-permute-start = (bf16[1,34,128,128]{3,2,1,0:T(8,128)(2,1)S(1)}, bf16[1,34,128,128]{3,2,1,0:T(8,128)(2,1)}, u32[]{:S(2)}, u32[]{:S(2)}) collective-permute-start(bf16[1,34,128,128]{3,2,1,0:T(8,128)(2,1)S(1)} %get-tuple-element.10), channel_id=1, source_target_pairs={{0,1},{1,2},{2,3},{3,4},{4,5},{5,6},{6,7},{7,8},{8,9},{9,10},{10,1... | collective-permute-start | bytes 3342344 | tf_op jit(solution)/shard_map/ppermute | solution.py:15
  45.8 4.6 %collective-permute-start.1 = (bf16[1,34,128,128]{3,2,1,0:T(8,128)(2,1)S(1)}, bf16[1,34,128,128]{3,2,1,0:T(8,128)(2,1)S(1)}, u32[]{:S(2)}, u32[]{:S(2)}) collective-permute-start(bf16[1,34,128,128]{3,2,1,0:T(8,128)(2,1)S(1)} %get-tuple-element.11), channel_id=1, source_target_pairs={{1,0},{2,1},{3,2},{4,3},{5,4},{6,5},{7,6},{8,7},{9,8},{10,9},{11,1... | collective-permute-start | bytes 3342344 | tf_op jit(solution)/shard_map/ppermute | solution.py:17
  50.5 1.0 copy-start.1
  141.2 4.1 %collective-permute-start.2 = (bf16[1,34,128,128]{3,2,1,0:T(8,128)(2,1)S(1)}, bf16[1,34,128,128]{3,2,1,0:T(8,128)(2,1)S(1)}, u32[]{:S(2)}, u32[]{:S(2)}) collective-permute-start(bf16[1,34,128,128]{3,2,1,0:T(8,128)(2,1)S(1)} %get-tuple-element.8), channel_id=1, source_target_pairs={{0,1},{1,2},{2,3},{3,4},{4,5},{5,6},{6,7},{7,8},{8,9},{9,10},{10,1... | collective-permute-start | bytes 3342344 | tf_op jit(solution)/shard_map/ppermute | solution.py:15
  143.0 4.8 %collective-permute-start.3 = (bf16[1,34,128,128]{3,2,1,0:T(8,128)(2,1)S(1)}, bf16[1,34,128,128]{3,2,1,0:T(8,128)(2,1)}, u32[]{:S(2)}, u32[]{:S(2)}) collective-permute-start(bf16[1,34,128,128]{3,2,1,0:T(8,128)(2,1)S(1)} %get-tuple-element.9), channel_id=1, source_target_pairs={{1,0},{2,1},{3,2},{4,3},{5,4},{6,5},{7,6},{8,7},{9,8},{10,9},{11,1... | collective-permute-start | bytes 3342344 | tf_op jit(solution)/shard_map/ppermute | solution.py:17
  145.3 1.1 copy-start.2
  241.4 2.0 copy-start
  243.7 5.0 %collective-permute-start.4 = (bf16[1,34,128,128]{3,2,1,0:T(8,128)(2,1)S(1)}, bf16[1,34,128,128]{3,2,1,0:T(8,128)(2,1)}, u32[]{:S(2)}, u32[]{:S(2)}) collective-permute-start(bf16[1,34,128,128]{3,2,1,0:T(8,128)(2,1)S(1)} %get-tuple-element.6), channel_id=1, source_target_pairs={{0,1},{1,2},{2,3},{3,4},{4,5},{5,6},{6,7},{7,8},{8,9},{9,10},{10,1... | collective-permute-start | bytes 3342344 | tf_op jit(solution)/shard_map/ppermute | solution.py:15
  246.5 4.8 %collective-permute-start.5 = (bf16[1,34,128,128]{3,2,1,0:T(8,128)(2,1)S(1)}, bf16[1,34,128,128]{3,2,1,0:T(8,128)(2,1)}, u32[]{:S(2)}, u32[]{:S(2)}) collective-permute-start(bf16[1,34,128,128]{3,2,1,0:T(8,128)(2,1)S(1)} %get-tuple-element.7), channel_id=1, source_target_pairs={{1,0},{2,1},{3,2},{4,3},{5,4},{6,5},{7,6},{8,7},{9,8},{10,9},{11,1... | collective-permute-start | bytes 3342344 | tf_op jit(solution)/shard_map/ppermute | solution.py:17
where the time goes:
time: 312 us
  blocking collectives  242 us (78%)
  matrix products  34.7 us (11%)
  starting transfers between devices  11 us (4%)
  local copies, waits for them, and re-layouts  8.78 us (3%)
  waiting for transfers between devices  8.28 us (3%)
  between operations  4.82 us (2%)
    psum x2, blocking collectives, shards(): alpha = lax.psum(jnp.sum(vector_f * image), 'site') / cells  97.3 us
    psum x2, blocking collectives, shards(): square = lax.psum(jnp.sum(residue * residue), 'site') / cells  60.2 us
    psum x1, blocking collectives, shards(): alpha_last = lax.psum(jnp.sum(vector_f * image), 'site') / cells  48.7 us
    psum x1, blocking collectives, shards(): scale = jnp.sqrt(lax.psum(jnp.sum(start * start), 'site') / cells + 1e-06)  35.5 us
    dot_general x3, matrix products, apply_h(): jnp.einsum('nwij,nwjk->nik', left_env, chosen, preferred_element_type=jnp...  23.7 us
    dot_general x3, matrix products, right_products(): jnp.einsum('nij,nwjk->nwik', vector, envir, preferred_element_type=jnp.fl...  10.9 us
    ppermute x3, waiting for transfers between devices, with_halo(): lax.ppermute(head, axis, [((i + 1) % count, i) for i in range(ends)])  7.15 us
    ppermute x3, starting transfers between devices, with_halo(): lax.ppermute(tail, axis, [(i, (i + 1) % count) for i in range(ends)])  6.98 us
  transfers between devices with their start and end apart: 6, of which 5 were waited for; matrix products, arithmetic and copies ran while one was open for 0% of the time, Pallas kernels for 0%

commit v1 on v0

v1 whole, which is shorter than its diff:
```python
import functools

import jax
import jax.numpy as jnp
from jax import lax
from jax.experimental import pallas as pl
from jax.experimental.pallas import tpu as pltpu
from jax.sharding import PartitionSpec as P

F32 = jnp.float32
BF16 = jnp.bfloat16
EPS = 1e-06


def kernel(
    n, cap, shift_ref, sizes_ref, psi_ref, left_hbm, right_hbm,
    kry_ref, img_ref, coef_ref,
    lbuf, rbuf, halo, pack, prod, where_at, nexts, u_ref, ue_ref, v_ref, ve_ref, live_ref,
    h_ref, t_ref, te_ref, part_ref, red_ref,
    load_sem, usend, urecv, hsend, hrecv, tsend, trecv, rsend, rrecv,
):
    sectors, width = psi_ref.shape[0], psi_ref.shape[1]
    count = shift_ref.shape[0]
    last = sectors - 1
    cells = float(n * sectors * width * width)
    me = lax.axis_index("site")
    has_left, has_right = me > 0, me < n - 1

    loads = []
    for i, (src, dst) in enumerate(((right_hbm, rbuf), (left_hbm, lbuf))):
        for a in range(sectors):
            copy = pltpu.make_async_copy(src.at[a], dst.at[pl.ds(a * count, count)], load_sem.at[i * sectors + a])
            copy.start()
            loads.append(copy)

    barrier = pltpu.get_barrier_semaphore()

    def greet(k, _):
        pl.semaphore_signal(
            barrier, inc=1, device_id={"site": lax.rem(me + k, n)}, device_id_type=pl.DeviceIdType.MESH
        )
        return 0

    lax.fori_loop(1, n, greet, 0)

    rows = lax.broadcasted_iota(jnp.int32, (width, width), 0)
    cols = lax.broadcasted_iota(jnp.int32, (width, width), 1)
    for a in range(sectors):
        keep = (rows < sizes_ref[a, 0]) & (cols < sizes_ref[a, 1])
        mask = jnp.where(keep, 1.0, 0.0).astype(F32)
        live_ref[a] = mask
        u_ref[a] = (psi_ref[a].astype(F32) * mask).astype(BF16)

    nl = jnp.int32(count)
    nr = jnp.int32(count)
    nexts[0, count] = nl
    nexts[1, count] = nr
    for w in range(count - 1, -1, -1):
        s = shift_ref[w]
        nexts[0, w] = nl
        nexts[1, w] = nr
        nl = jnp.where(s == -1, w, nl)
        nr = jnp.where(s == 1, w, nr)
    low = jnp.int32(sectors * count)
    high = jnp.int32(sectors * count + cap)
    for w in range(count):
        s = shift_ref[w]
        for a in range(sectors):
            place = (a + s) * count + w
            if a == 0:
                place = jnp.where(s == -1, low, place)
            if a == last:
                place = jnp.where(s == 1, high, place)
            where_at[a, w] = place
        low = low + jnp.where(s == -1, 1, 0)
        high = high + jnp.where(s == 1, 1, 0)

    @pl.when(me == 0)
    def _():
        ue_ref[0] = jnp.zeros((width, width), BF16)
        te_ref[0, 0] = jnp.zeros((width, width), F32)
        te_ref[1, 0] = jnp.zeros((width, width), F32)
        halo[0] = jnp.zeros((cap, width, width), BF16)

    @pl.when(me == n - 1)
    def _():
        ue_ref[1] = jnp.zeros((width, width), BF16)
        te_ref[0, 1] = jnp.zeros((width, width), F32)
        te_ref[1, 1] = jnp.zeros((width, width), F32)
        halo[1] = jnp.zeros((cap, width, width), BF16)

    def remote(src, dst, ssem, rsem, to):
        return pltpu.make_async_remote_copy(
            src_ref=src, dst_ref=dst, send_sem=ssem, recv_sem=rsem,
            device_id={"site": to}, device_id_type=pl.DeviceIdType.MESH,
        )

    def swap(first_src, last_src, dst, ssem, rsem):
        right = remote(last_src, dst.at[0], ssem.at[0], rsem.at[0], jnp.minimum(me + 1, n - 1))
        left = remote(first_src, dst.at[1], ssem.at[1], rsem.at[1], jnp.maximum(me - 1, 0))
        return right, left

    def start(pair):
        pl.when(has_right)(lambda: pair[0].start())
        pl.when(has_left)(lambda: pair[1].start())

    def finish(pair):
        @pl.when(has_left)
        def _():
            pair[0].wait_recv()
            pair[1].wait_send()

        @pl.when(has_right)
        def _():
            pair[1].wait_recv()
            pair[0].wait_send()

    pl.semaphore_wait(barrier, n - 1)
    u_pair = swap(u_ref.at[0], u_ref.at[last], ue_ref, usend, urecv)
    start(u_pair)

    for copy in loads[:sectors]:
        copy.wait()

    def packing(j, at):
        at_low, at_high = at
        pack[0, j] = rbuf[last * count + jnp.minimum(at_low, count - 1)]
        pack[1, j] = rbuf[jnp.minimum(at_high, count - 1)]
        return nexts[0, at_low], nexts[1, at_high]

    lax.fori_loop(0, cap, packing, (nl, nr))
    halo_pair = swap(pack.at[1], pack.at[0], halo, hsend, hrecv)
    start(halo_pair)

    group = 2 if count % 2 == 0 and cap % 2 == 0 else 1

    def products(vector, envir, base, first):
        rhs = [envir[base + first + i] for i in range(group)]
        rhs = rhs[0] if group == 1 else jnp.concatenate(rhs, axis=1)
        return jnp.dot(vector, rhs, preferred_element_type=F32).astype(BF16)

    def local_products(vec):
        def body(p, _):
            for b in range(sectors):
                out = products(vec[b], rbuf, b * count, p * group)
                for i in range(group):
                    prod[b * count + p * group + i] = out[:, i * width : (i + 1) * width]
            return 0

        lax.fori_loop(0, count // group, body, 0)

    def halo_products(vec):
        def body(p, _):
            for side in range(2):
                out = products(vec[side], halo.at[side], 0, p * group)
                for i in range(group):
                    prod[sectors * count + side * cap + p * group + i] = out[:, i * width : (i + 1) * width]
            return 0

        lax.fori_loop(0, cap // group, body, 0)

    chunk = count // 2 if count % 2 == 0 else count

    def left_side(c, _):
        for a in range(sectors):
            lhs = jnp.concatenate([lbuf[a * count + c * chunk + i] for i in range(chunk)], axis=1)
            rhs = jnp.concatenate([prod[where_at[a, c * chunk + i]] for i in range(chunk)], axis=0)
            out = jnp.dot(lhs, rhs, preferred_element_type=F32)
            h_ref[a] = h_ref[a] + out * live_ref[a]
        return 0

    def apply_left():
        h_ref[...] = jnp.zeros_like(h_ref)
        lax.fori_loop(0, count // chunk, left_side, 0)

    def flat(x):
        return x.reshape(sectors * width, width)

    def lanes(x):
        return jnp.sum(x, axis=0, keepdims=True)

    def reduce_start(step, sums):
        part_ref[step] = jnp.concatenate(
            sums + [jnp.zeros((8 - len(sums), width), F32)], axis=0
        )
        red_ref[step, me] = part_ref[step]

        def send(k, _):
            remote(
                part_ref.at[step], red_ref.at[step, me], rsend.at[step, k], rrecv.at[step, me],
                lax.rem(me + k, n),
            ).start()
            return 0

        lax.fori_loop(1, n, send, 0)

    def reduce_finish(step):
        def wait(k, _):
            j = lax.rem(me + k, n)
            got = remote(part_ref.at[step], red_ref.at[step, j], rsend.at[step, k], rrecv.at[step, j], j)
            got.wait_recv()
            got.wait_send()
            return 0

        lax.fori_loop(1, n, wait, 0)
        return [red_ref[step, :, q, :] for q in range(4)]

    def total(x):
        return jnp.sum(jnp.sum(x, axis=0, keepdims=True), axis=1, keepdims=True) / cells

    def ratio(top, bottom):
        return jnp.where(bottom > 0.0, top / jnp.where(bottom > 0.0, bottom, 1.0), 0.0)

    local_products(u_ref)
    for copy in loads[sectors:]:
        copy.wait()
    finish(u_pair)
    finish(halo_pair)
    halo_products(ue_ref)
    apply_left()
    t_pair = swap(h_ref.at[0], h_ref.at[last], te_ref.at[0], tsend.at[0], trecv.at[0])
    start(t_pair)
    u = flat(u_ref[...]).astype(F32)
    g = flat(h_ref[...])
    uu, ug = lanes(u * u), lanes(u * g)
    r = g - ratio(ug, uu) * u
    reduce_start(0, [uu, ug, lanes(r * r)])
    uu, ug, rr, _ = reduce_finish(0)
    scale2 = total(uu) + EPS
    inv_scale = lax.rsqrt(scale2)
    alpha1 = total(ug) / scale2
    off = ratio(ug, uu) - alpha1
    beta1 = jnp.sqrt(total(rr + off * off * uu) / scale2 + EPS)
    down = inv_scale / beta1
    finish(t_pair)
    for a in range(sectors):
        v_ref[a] = ((h_ref[a] - alpha1 * u_ref[a].astype(F32)) * down).astype(BF16)
    for side in range(2):
        ve_ref[side] = ((te_ref[0, side] - alpha1 * ue_ref[side].astype(F32)) * down).astype(BF16)

    local_products(v_ref)
    halo_products(ve_ref)
    apply_left()
    v = flat(v_ref[...]).astype(F32)
    h = flat(h_ref[...])
    t = h - (beta1 * inv_scale) * flat(u_ref[...]).astype(F32)
    t_ref[...] = t.reshape(t_ref.shape)
    t_pair = swap(t_ref.at[0], t_ref.at[last], te_ref.at[1], tsend.at[1], trecv.at[1])
    start(t_pair)
    vv, vh, vt = lanes(v * v), lanes(v * h), lanes(v * t)
    r = t - ratio(vt, vv) * v
    reduce_start(1, [vv, vh, vt, lanes(r * r)])
    vv, vh, vt, rr = reduce_finish(1)
    alpha2 = total(vh)
    off = ratio(vt, vv) - alpha2
    beta2 = jnp.sqrt(total(rr + off * off * vv) + EPS)
    down = 1.0 / beta2
    finish(t_pair)
    for a in range(sectors):
        kry_ref[a] = ((t_ref[a] - alpha2 * v_ref[a].astype(F32)) * down).astype(BF16)
    for side in range(2):
        ve_ref[side] = ((te_ref[1, side] - alpha2 * ve_ref[side].astype(F32)) * down).astype(BF16)

    local_products(kry_ref)
    halo_products(ve_ref)
    apply_left()
    reduce_start(2, [lanes(flat(kry_ref[...]).astype(F32) * flat(h_ref[...]))])
    img_ref[...] = h_ref[...].astype(BF16)
    alpha3 = total(reduce_finish(2)[0])
    lane = lax.broadcasted_iota(jnp.int32, coef_ref.shape, 1)
    out = jnp.zeros(coef_ref.shape, F32)
    for i, value in enumerate((alpha1, alpha2, alpha3, beta1, beta2)):
        out = jnp.where(lane == i, value, out)
    coef_ref[...] = out


def call(n, cap, collective, psi, left_env, right_env, mpo_shift, block_sizes):
    sectors, width = psi.shape[0], psi.shape[1]
    count = mpo_shift.shape[0]
    vmem = pl.BlockSpec(memory_space=pltpu.VMEM)
    smem = pl.BlockSpec(memory_space=pltpu.SMEM)
    hbm = pl.BlockSpec(memory_space=pl.ANY)
    block = (width, width)
    dma = pltpu.SemaphoreType.DMA
    return pl.pallas_call(
        functools.partial(kernel, n, cap),
        out_shape=(
            jax.ShapeDtypeStruct(psi.shape, BF16),
            jax.ShapeDtypeStruct(psi.shape, BF16),
            jax.ShapeDtypeStruct((1, width), F32),
        ),
        in_specs=[smem, smem, vmem, hbm, hbm],
        out_specs=(vmem, vmem, vmem),
        scratch_shapes=[
            pltpu.VMEM((sectors * count,) + block, BF16),
            pltpu.VMEM((sectors * count,) + block, BF16),
            pltpu.VMEM((2, cap) + block, BF16),
            pltpu.VMEM((2, cap) + block, BF16),
            pltpu.VMEM((sectors * count + 2 * cap,) + block, BF16),
            pltpu.SMEM((sectors, count), jnp.int32),
            pltpu.SMEM((2, count + 1), jnp.int32),
            pltpu.VMEM((sectors,) + block, BF16),
            pltpu.VMEM((2,) + block, BF16),
            pltpu.VMEM((sectors,) + block, BF16),
            pltpu.VMEM((2,) + block, BF16),
            pltpu.VMEM((sectors,) + block, F32),
            pltpu.VMEM((sectors,) + block, F32),
            pltpu.VMEM((sectors,) + block, F32),
            pltpu.VMEM((2, 2) + block, F32),
            pltpu.VMEM((3, 8, width), F32),
            pltpu.VMEM((3, n, 8, width), F32),
            dma((2 * sectors,)),
            dma((2,)), dma((2,)), dma((2,)), dma((2,)),
            dma((2, 2)), dma((2, 2)),
            dma((3, n)), dma((3, n)),
        ],
        compiler_params=pltpu.CompilerParams(
            collective_id=collective, has_side_effects=True, vmem_limit_bytes=56 * 1024 * 1024
        ),
    )(mpo_shift, block_sizes, psi, left_env, right_env)


def shards(n, psi, left_env, right_env, mpo_shift, block_sizes):
    count = mpo_shift.shape[0]
    krylov, image, coefficients = call(n, count, 0, psi, left_env, right_env, mpo_shift, block_sizes)
    return krylov, image, coefficients[0, :5]


def solution(mesh):
    in_specs = (
        P(("grp", "site"), None, None),
        P(("grp", "site"), None, None, None),
        P(("grp", "site"), None, None, None),
        P(),
        P(("grp", "site"), None),
    )
    out_specs = (P(("grp", "site"), None, None), P(("grp", "site"), None, None), P("grp"))
    return jax.shard_map(
        functools.partial(shards, mesh.shape["site"]),
        mesh=mesh, in_specs=in_specs, out_specs=out_specs, check_vma=False,
    )
```

time: 312 us -> 77.1 us (0.25)
  blocking collectives: 242 us -> 0 us
  Pallas kernels: 0 us -> 70.7 us
  matrix products: 34.7 us -> 0 us
  starting transfers between devices: 11 us -> 0 us
  waiting for transfers between devices: 8.28 us -> 0 us
  between operations: 4.82 us -> 0.64 us
  local copies, waits for them, and re-layouts: 8.78 us -> 5.6 us
    psum x6 -> x0, blocking collectives: 242 us -> none  [the longest x2 97.3 us: shards(): alpha = lax.psum(jnp.sum(vector_f * image), 'site') / cells]
    pallas_call x0 -> x1, Pallas kernels: none -> 70.7 us  [call(): pl.pallas_call(functools.partial(kernel, n, cap), out_shape=(jax.ShapeDty...]
    dot_general x6 -> x0, matrix products: 34.7 us -> none  [the longest x3 23.7 us: apply_h(): jnp.einsum('nwij,nwjk->nik', left_env, chosen, preferred_element_type=jnp...]
    ppermute x6 -> x0, starting transfers between devices: 11 us -> none  [the longest x3 6.98 us: with_halo(): lax.ppermute(tail, axis, [(i, (i + 1) % count) for i in range(ends)])]
    ppermute x6 -> x0, waiting for transfers between devices: 8.28 us -> none  [the longest x3 7.15 us: with_halo(): lax.ppermute(head, axis, [((i + 1) % count, i) for i in range(ends)])]
    unnamed x11 -> x3, local copies, waits for them, and re-layouts: 6.64 us -> 4.47 us
  transfers between devices with their start and end apart: 6 -> 0, of which waited for: 5 -> 0; matrix products, arithmetic and copies ran while one was open for 0% -> 0% of each run, Pallas kernels for 0% -> 0%
where the time goes in v1:
time: 77.1 us; the launch traced here: 76.9 us
  Pallas kernels  70.7 us (92%)
  local copies, waits for them, and re-layouts  5.6 us (7%)
    pallas_call x1, Pallas kernels, call(): pl.pallas_call(functools.partial(kernel, n, cap), out_shape=(jax.ShapeDty...  70.7 us
    unnamed x3, local copies, waits for them, and re-layouts  4.47 us

profile of v1, /device:TPU:0, one launch (start us, length us, event | category | flops | bytes accessed | tf_op | source)
XLA Modules:
  0.0 76.9 jit_solution(14591166607693453528)
XLA Ops:
  0.6 1.3 %copy.8.sizes_ref = s32[4,2]{1,0:T(4,128)} copy(s32[4,2]{0,1:T(2,128)} %param.9) | data formatting | bytes 64 | tf_op args[4]
  2.0 70.7 %shard_map.76 = (bf16[4,128,128]{2,1,0:T(8,128)(2,1)}, bf16[4,128,128]{2,1,0:T(8,128)(2,1)}, f32[1,128]{1,0:T(1,128)}) custom-call(s32[34]{0:T(128)} %shift_ref.1, s32[4,2]{1,0:T(4,128)} %copy.8.sizes_ref, bf16[4,128,128]{2,1,0:T(8,128)(2,1)} %psi_ref.1, bf16[4,34,128,128]{3,2,1,0:T(8,128)(2,1)} %left_hbm.1, bf16[4,34,128,128]{3,2,1,0:T(8,128)(2,1)} %right_hbm.1), custom_call_target="tpu_custom_call" | custom-call | tf_op jit(solution)/shard_map/pallas_call | solution.py:285
  72.6 1.1 %slice_bitcast_fusion = f32[5]{0:T(128)} fusion(f32[1,128]{1,0:T(1,128)} %get-tuple-element.8), kind=kLoop, calls=%fused_computation | loop fusion | bytes 40 | tf_op jit(solution)/shard_map/squeeze | solution.py:326
  73.8 1.6 %copy.11 = bf16[4,128,128]{2,1,0:T(8,128)(2,1)} copy(bf16[4,128,128]{2,1,0:T(8,128)(2,1)} %get-tuple-element.12) | data formatting | bytes 262144
  75.3 1.6 %copy.12 = bf16[4,128,128]{2,1,0:T(8,128)(2,1)} copy(bf16[4,128,128]{2,1,0:T(8,128)(2,1)} %get-tuple-element.13) | data formatting | bytes 262144
